TPU v7x, 256 devices: a whole 4x4x8 slice. The times are simulated.
256 devices in a mesh: dp: 8 (over z), graph: 32 (over x, y, core).
Axes of the slice: x: 4, y: 4, z: 8, core: 2. Of those that a mesh axis runs over, the one named last changes fastest.
Arguments:
- node_feats: bfloat16 [8, 224, 49, 256], P('dp', 'graph'), may hold values from -0.125 to 0.125
- node_grads: bfloat16 [8, 224, 49, 256], P('dp', 'graph'), may hold values from -1.75 to 1.75
- node_row: int32 [8, 224], P('dp'), may hold values from 0 to 223, as said below
- edge_src: int32 [8, 16384], P('dp', 'graph'), may hold values from 0 to 223, as said below
- edge_tgt: int32 [8, 16384], P('dp', 'graph'), may hold values from 0 to 223, as said below
- edge_rot: int32 [8, 16384], P('dp', 'graph'), may hold values from 0 to 2047
- edge_len: float32 [8, 16384], P('dp', 'graph'), may hold values from 0.5 to 11.5
- edge_count: int32 [8, 32], P('dp', 'graph'), may hold values from 64 to 512, as said below
- rotations: bfloat16 [2048, 7, 49], replicated, as said below
- w_zero: bfloat16 [1792, 1792], replicated, may hold values from -0.125 to 0.125
- w_radial: float32 [600, 256], replicated, may hold values from -3 to 3
Outputs:
- node_grad: float32 [8, 224, 49, 256], P('dp', 'graph')
- weight_grad: float32 [1792, 1792], P('graph')
Inputs may be any that keep to these rules, and one draw needn't show every extreme that they name: Each row of node_row is a permutation: atom i of a batch graph is held at row node_row[b, i], and graph index g holds rows g * 7 to (g + 1) * 7 - 1. `edge_tgt`: for every slot of the block of graph index g, the target atom is held at one of the rows g * 7 to (g + 1) * 7 - 1. `edge_src`: among the 512 slots of the block of one index of graph, at most 24 have source atoms held by the same index of graph; in every batch graph one index of graph holds the source atoms of exactly 24 live slots of every block. The first edge_count[b, g] slots of a block are live, the others are padding with valid ids; in every batch graph one index of graph has all 512 slots live. `rotations`: row l of each rotation is zero outside the coefficients of degree l (coefficients l * l to l * l + 2 l).
All inputs are finite; a program needn't handle non-finite values.
Results may differ from a plain program's by a relative error of at most 0.0041.
Values may be sent and summed in bfloat16 or wider, within the bound.
A program may use at most 256 MiB of HBM per device.

v0:
```python
import jax
import jax.numpy as jnp
from jax import lax
from jax.sharding import PartitionSpec as P

BLOCK = 256
CUTOFF = 12.0


def radial_profile(lengths, w_radial):
    gauss_count = w_radial.shape[0]
    spacing = CUTOFF / (gauss_count - 1)
    centers = jnp.arange(gauss_count).astype(jnp.float32) * spacing
    basis = jnp.exp(-0.5 / (2.0 * spacing) ** 2 * (lengths[:, None] - centers[None, :]) ** 2)
    return jnp.dot(
        basis, w_radial, precision=lax.Precision.HIGHEST, preferred_element_type=jnp.float32
    )


def find_rows(atom_ids, row_table):
    matches = atom_ids[:, None] == jnp.arange(row_table.shape[0], dtype=jnp.int32)[None, :]
    return jnp.sum(jnp.where(matches, row_table[None, :], 0), axis=1)


def forward_rows(turning, source, radial):
    rotated = jnp.einsum("bij,bjc->bic", turning, source, preferred_element_type=jnp.float32)
    return (rotated * radial[:, None, :]).astype(jnp.bfloat16)


def backward_terms(edge_in, target, turning, radial, w_zero):
    edge_grad = jnp.einsum(
        "bij,bjc->bic", turning, target, preferred_element_type=jnp.float32
    ).astype(jnp.bfloat16)
    edge_rows = edge_in.shape[0]
    flat_in = edge_in.reshape(edge_rows, -1)
    flat_grad = edge_grad.reshape(edge_rows, -1)
    weight_term = lax.dot_general(
        flat_in, flat_grad, (((0,), (0,)), ((), ())), preferred_element_type=jnp.float32
    )
    hidden = lax.dot_general(
        flat_grad, w_zero, (((1,), (1,)), ((), ())), preferred_element_type=jnp.float32
    )
    returned = (hidden.reshape(edge_in.shape) * radial[:, None, :]).astype(jnp.bfloat16)
    return (weight_term, returned)


def spread_back(turning, returned):
    return jnp.einsum("bij,bic->bjc", turning, returned, preferred_element_type=jnp.float32)


def per_device(
    node_feats,
    node_grads,
    node_row,
    edge_src,
    edge_tgt,
    edge_rot,
    edge_len,
    edge_count,
    rotations,
    w_zero,
    w_radial,
):
    node_dev = node_feats.shape[1]
    own_index = lax.axis_index("graph")
    row_table = node_row[0]
    grad_table = node_grads[0]
    source_ids = edge_src[0]
    target_rows = find_rows(edge_tgt[0], row_table) - own_index * node_dev
    turn_ids = edge_rot[0]
    lengths = edge_len[0]
    live_count = edge_count[0, 0]
    source_rows = find_rows(source_ids, row_table)
    square = w_zero.shape[0]
    blocks = (live_count + BLOCK - 1) // BLOCK
    sources_all = lax.all_gather(node_feats, "graph", axis=1, tiled=True)[0]

    def advance(step_index, carry):
        weight_acc, node_acc = carry
        first = step_index * BLOCK
        here_source = lax.dynamic_slice_in_dim(source_rows, first, BLOCK)
        here_target = lax.dynamic_slice_in_dim(target_rows, first, BLOCK)
        here_turn = lax.dynamic_slice_in_dim(turn_ids, first, BLOCK)
        here_length = lax.dynamic_slice_in_dim(lengths, first, BLOCK)
        alive_mask = (first + jnp.arange(BLOCK, dtype=jnp.int32) < live_count).astype(jnp.float32)
        radial = radial_profile(here_length, w_radial) * alive_mask[:, None]
        turning = rotations[here_turn]
        edge_in = forward_rows(turning, sources_all[here_source], radial)
        weight_term, returned = backward_terms(
            edge_in, grad_table[here_target], turning, radial, w_zero
        )
        return (
            weight_acc + weight_term,
            node_acc.at[here_source].add(spread_back(turning, returned)),
        )

    start_state = (
        jnp.zeros((square, square), jnp.float32),
        jnp.zeros(sources_all.shape, jnp.float32),
    )
    weight_acc, node_acc = lax.fori_loop(0, blocks, advance, start_state)
    node_part = lax.psum_scatter(node_acc[None], "graph", scatter_dimension=1, tiled=True)
    rows_part = lax.psum_scatter(weight_acc, "graph", scatter_dimension=0, tiled=True)
    weight_grad = lax.psum(rows_part, "dp")
    return (node_part, weight_grad)


def solution(mesh):
    placed = (
        P("dp", "graph", None, None),
        P("dp", "graph", None, None),
        P("dp", None),
        P("dp", "graph"),
        P("dp", "graph"),
        P("dp", "graph"),
        P("dp", "graph"),
        P("dp", "graph"),
        P(),
        P(),
        P(),
    )
    return jax.shard_map(
        per_device,
        mesh=mesh,
        in_specs=placed,
        out_specs=(P("dp", "graph", None, None), P("graph", None)),
        check_vma=False,
    )
```

profile of v0, /device:TPU:2, one launch (start us, length us, event | category | flops | bytes accessed | tf_op | source)
XLA Modules:
  0.0 616.0 jit_solution(6712216942642518904)
XLA Ops:
  7.2 0.7 all-gather.2.cloned.1.call-update
  8.6 5.6 copy.34
  14.2 0.9 select_reduce_fusion
  15.1 52.0 %all-gather.2.cloned.1.call-done = bf16[1,224,49,256]{3,2,0,1:T(8,128)(2,1)} async-done(((bf16[1,7,49,256]{3,2,0,1:T(8,128)(2,1)}), bf16[1,224,49,256]{3,2,0,1:T(8,128)(2,1)}) %all-gather.2.cloned.1.call-update) | async-done | bytes 5619728 | tf_op jit(solution)/shard_map/all_gather | solution.py:76
  67.1 5.5 broadcast_in_dim.44
  72.6 5.4 broadcast_in_dim.45
  78.1 100.3 %while.12 = (s32[]{:T(128)}, f32[1792,1792]{1,0:T(8,128)}, f32[224,49,256]{2,1,0:T(8,128)}, s32[]{:T(128)}, s32[512]{0:T(512)S(1)}, /*index=5*/bf16[2048,7,49]{2...) while((s32[]{:T(128)}, f32[1792,1792]{1,0:T(8,128)}, ...), condition=%wide.region_4.5_spmd, body=%wide.region_2.4_spmd.sunk | while | flops 3904316672 | bytes 142397968 | solution.py:101
  78.3 0.1 compare_select_fusion.5
  78.4 3.0 gather_fusion
  81.4 0.1 compare_select_fusion.6
  81.5 6.8 %gather_fusion.1 = bf16[256,49,256]{2,1,0:T(8,128)(2,1)} fusion(bf16[224,49,256]{2,1,0:T(8,128)(2,1)} %get-tuple-element.287, s32[1024]{0:T(1024)S(1)} %pad_clamp_fusion.7), kind=kCustom, calls=%fused_computation.1.clone.1 | custom fusion | bytes 12846080 | tf_op jit(solution)/shard_map/while/body/gather | solution.py:88
  88.3 0.1 dynamic_slice.20
  88.4 0.6 compare_convert_fusion.2
  89.0 0.9 convolution_multiply_fusion.2
  89.9 4.4 multiply_convert_fusion.2
  94.4 0.8 copy.49
  95.2 4.0 gather_fusion.2
  99.2 4.4 convolution_convert_fusion.2
  103.6 1.6 copy.50
  105.1 11.9 %convolution_add_fusion.2 = f32[1792,1792]{1,0:T(8,128)} fusion(f32[1792,1792]{1,0:T(8,128)} %get-tuple-element.263, bf16[256,1792]{0,1:T(8,128)(2,1)S(1)} %bitcast.58, bf16[256,1792]{0,1:T(8,128)(2,1)} %bitcast.59), kind=kOutput, calls=%fused_computation.4.clone.1 | convolution fusion | flops 1647378432 | bytes 27525120 | tf_op jit(solution)/shard_map/while/body/dot_general | solution.py:37
  117.0 4.7 fusion.49
  121.7 7.3 %fusion.50 = f32[256,49,256]{2,1,0:T(8,128)} fusion(bf16[256,7,49]{2,1,0:T(8,128)(2,1)S(1)} %gather_fusion, f32[256,7,256]{2,0,1:T(8,128)S(1)} %fusion.49, f32[256,256]{1,0:T(8,128)S(1)} %convolution_multiply_fusion.2), kind=kOutput, calls=%fused_computation.10.clone.1 | convolution fusion | flops 45875200 | bytes 15117824 | tf_op jit(solution)/shard_map/while/body/bij,bic->bjc/dot_general | solution.py:48
  129.1 49.3 %scatter_fusion = f32[224,49,256]{2,1,0:T(8,128)} fusion(f32[224,49,256]{2,1,0:T(8,128)} %get-tuple-element.264, s32[256]{0:T(256)S(1)} %get-tuple-element.242, f32[256,49,256]{2,1,0:T(8,128)} %fusion.50), kind=kCustom, calls=%fused_computation.3.clone.1 | custom fusion | flops 3211264 | bytes 38536192 | tf_op jit(solution)/shard_map/while/body/scatter-add | solution.py:94
  178.3 0.0 all-reduce.6.cloned.1.call-start
  178.4 14.6 %copy.36 = f32[1,224,49,256]{3,0,2,1:T(1,128)} copy(f32[1,224,49,256]{3,2,1,0:T(8,128)} %bitcast.56) | data formatting | bytes 22478848 | tf_op jit(solution)/shard_map/broadcast_in_dim | solution.py:102
  193.0 0.0 all-reduce.4.cloned.1.call-start
  193.1 197.9 %reduce-scatter.2.cloned.1.call-done = f32[56,1792]{1,0:T(8,128)} async-done(((f32[1792,1792]{1,0:T(8,128)}), f32[56,1792]{1,0:T(8,128)}) %reduce-scatter.2.cloned.1.call-update) | async-done | bytes 401424 | tf_op jit(solution)/shard_map/reduce_scatter | solution.py:103
  391.0 0.6 dynamic-slice
  392.2 140.3 %all-reduce.6.cloned.1.call-done = f32[1,224,49,256]{3,0,2,1:T(1,128)} async-done(((f32[1,224,49,256]{3,0,2,1:T(1,128)}), f32[1,224,49,256]{3,0,2,1:T(1,128)}) %all-reduce.6.cloned.1.call-update) | async-done | bytes 11239440
  532.5 2.0 constant_dynamic-slice_fusion
  534.4 73.3 %all-reduce.4.cloned.1.call-done = f32[56,1792]{1,0:T(8,128)} async-done(((f32[56,1792]{1,0:T(8,128)}), f32[56,1792]{1,0:T(8,128)}) %all-reduce.4.cloned.1.call-update) | async-done | bytes 401424 | tf_op jit(solution)/shard_map/psum | solution.py:104
  607.7 1.8 copy.64
  (24 shorter events, 0.2 us)
Async XLA Ops:
  7.2 59.9 %all-gather.2.cloned.1.call-start = ((), (), s32[]{:S(2)}) async-start(), calls=%async_computation.1 | async-start | bytes 6623232 | tf_op jit(solution)/shard_map/all_gather | solution.py:76
  7.9 383.0 %reduce-scatter.2.cloned.1.call-start = ((), (), s32[]{:S(2)}) async-start(), calls=%async_computation.2 | async-start | bytes 13246464 | tf_op jit(solution)/shard_map/reduce_scatter | solution.py:103
  72.6 5.4 copy-start
  72.6 5.4 copy-start.2
  72.6 5.4 copy-start.3
  72.6 5.4 copy-start.4
  105.1 11.9 %copy-start.1 = (bf16[256,7,256]{0,2,1:T(8,128)(2,1)S(1)}, bf16[256,7,256]{0,2,1:T(8,128)(2,1)}, u32[]{:S(2)}) copy-start(bf16[256,7,256]{0,2,1:T(8,128)(2,1)} %copy.50) | copy-start | bytes 2752516 | tf_op jit(solution)/shard_map/while
  129.0 49.3 %copy-start.5 = (f32[600,256]{1,0:T(8,128)S(1)}, f32[600,256]{1,0:T(8,128)}, u32[]{:S(2)}) copy-start(f32[600,256]{1,0:T(8,128)} %get-tuple-element.334) | copy-start | bytes 1843204 | tf_op jit(solution)/shard_map/while
  178.3 354.2 %all-reduce.6.cloned.1.call-start = ((), (), s32[]{:S(2)}) async-start(), calls=%async_computation.4 | async-start | bytes 22478848
  193.0 198.0 %copy-start.6 = (u32[256]{0:T(256)S(1)}, u32[256]{0:T(256)}, u32[]{:S(2)}) copy-start(u32[256]{0:T(256)} %constant.58) | copy-start | bytes 3076
  193.0 414.7 %all-reduce.4.cloned.1.call-start = ((), (), s32[]{:S(2)}) async-start(), calls=%async_computation.3 | async-start | bytes 802816 | tf_op jit(solution)/shard_map/psum | solution.py:104
Sparse Core Ops, SparseCore 0:
  10.6 56.4 all-gather.1
  178.5 212.4 reduce-scatter.1
  394.4 137.9 all-reduce.5
  534.7 72.9 all-reduce.3
where the time goes:
time: 618 us; the launch traced here: 616 us
  waiting for transfers between devices  464 us (75%)
  local copies, waits for them, and re-layouts  51.7 us (8%)
  other arithmetic  51 us (8%)
  matrix products  33.7 us (5%)
  between operations  15.1 us (2%)
    reduce_scatter x1, waiting for transfers between devices, per_device(): lax.psum_scatter(weight_acc, 'graph', scatter_dimension=0, tiled=True)  198 us
    unnamed x5, waiting for transfers between devices  141 us
    psum x1, waiting for transfers between devices, per_device(): weight_grad = lax.psum(rows_part, 'dp')  73.3 us
    all_gather x1, waiting for transfers between devices, per_device(): sources_all = lax.all_gather(node_feats, 'graph', axis=1, tiled=True)[0]  52 us
    scatter-add x1, other arithmetic, advance(): node_acc.at[here_source].add(spread_back(turning, returned))  49.3 us
    broadcast_in_dim x1, local copies, waits for them, and re-layouts, per_device(): node_acc[None]  14.6 us
  transfers between devices with their start and end apart: 4, of which 4 were waited for; matrix products, arithmetic and copies ran while one was open for 4% of the time, Pallas kernels for 0%

commit v1 on v0

--- a/solution.py
+++ b/solution.py
@@ -73,7 +73,9 @@
     source_rows = find_rows(source_ids, row_table)
     square = w_zero.shape[0]
     blocks = (live_count + BLOCK - 1) // BLOCK
-    sources_all = lax.all_gather(node_feats, "graph", axis=1, tiled=True)[0]
+    sources_all = jnp.concatenate(
+        lax.all_to_all(jnp.stack([node_feats] * lax.axis_size("graph")), "graph", 0, 0), axis=1
+    )[0]
 
     def advance(step_index, carry):
         weight_acc, node_acc = carry

time: 618 us -> 665 us (1.076)
  waiting for transfers between devices: 464 us -> 502 us
  starting transfers between devices: 0.16 us -> 7.94 us
    all_to_all x0 -> x1, waiting for transfers between devices: none -> 73.9 us  [per_device(): lax.all_to_all(jnp.stack([node_feats] * lax.axis_size('graph')), 'graph',...]
    all_gather x1 -> x0, waiting for transfers between devices: 52 us -> none  [per_device(): sources_all = lax.all_gather(node_feats, 'graph', axis=1, tiled=True)[0]]
    reduce_scatter x1, waiting for transfers between devices: 198 us -> 214 us  [per_device(): lax.psum_scatter(weight_acc, 'graph', scatter_dimension=0, tiled=True)]
    all_to_all x0 -> x1, starting transfers between devices: none -> 7.81 us  [per_device(): lax.all_to_all(jnp.stack([node_feats] * lax.axis_size('graph')), 'graph',...]
    unnamed x5 -> x4, waiting for transfers between devices: 141 us -> 140 us
  transfers between devices with their start and end apart: 4 -> 4, of which waited for: 4 -> 4; matrix products, arithmetic and copies ran while one was open for 4% -> 3% of each run, Pallas kernels for 0% -> 0%
where the time goes in v1:
time: 665 us; the launch traced here: 664 us
  waiting for transfers between devices  502 us (75%)
  local copies, waits for them, and re-layouts  54.4 us (8%)
  other arithmetic  50.4 us (8%)
  matrix products  33.7 us (5%)
  between operations  15.1 us (2%)
  starting transfers between devices  7.94 us (1%)
    reduce_scatter x1, waiting for transfers between devices, per_device(): lax.psum_scatter(weight_acc, 'graph', scatter_dimension=0, tiled=True)  214 us
    unnamed x4, waiting for transfers between devices  140 us
    all_to_all x1, waiting for transfers between devices, per_device(): lax.all_to_all(jnp.stack([node_feats] * lax.axis_size('graph')), 'graph',...  73.9 us
    psum x1, waiting for transfers between devices, per_device(): weight_grad = lax.psum(rows_part, 'dp')  73.4 us
    scatter-add x1, other arithmetic, advance(): node_acc.at[here_source].add(spread_back(turning, returned))  49.3 us
    broadcast_in_dim x1, local copies, waits for them, and re-layouts, per_device(): node_acc[None]  14.6 us
  transfers between devices with their start and end apart: 4, of which 4 were waited for; matrix products, arithmetic and copies ran while one was open for 3% of the time, Pallas kernels for 0%

profile of v1, /device:TPU:2, one launch (start us, length us, event | category | flops | bytes accessed | tf_op | source)
XLA Modules:
  0.0 663.5 jit_solution(4338574165665267632)
XLA Ops:
  7.2 4.0 stack.2
  11.2 7.8 %all-to-all-start = ((bf16[32,1,7,49,256]{4,3,2,1,0:T(8,128)(2,1)}), bf16[32,1,7,49,256]{4,3,2,1,0:T(8,128)(2,1)}, u32[]{:S(2)}, u32[]{:S(2)}) async-start(bf16[32,1,7,49,256]{4,3,2,1,0:T(8,128)(2,1)} %stack.2), calls=%async_computation | async-start | bytes 12845056 | tf_op jit(solution)/shard_map/all_to_all | solution.py:77
  19.8 4.2 copy.32
  24.0 0.2 select_reduce_fusion
  24.2 73.9 %all-to-all-done = bf16[32,1,7,49,256]{4,3,2,1,0:T(8,128)(2,1)} async-done(((bf16[32,1,7,49,256]{4,3,2,1,0:T(8,128)(2,1)}), bf16[32,1,7,49,256]{4,3,2,1,0:T(8,128)(2,1)}, u32[]{:S(2)}, u32[]{:S(2)}) %all-to-all-start) | async-done | bytes 5619744 | tf_op jit(solution)/shard_map/all_to_all | solution.py:77
  98.1 5.5 broadcast_in_dim.44
  103.7 5.4 broadcast_in_dim.45
  109.1 100.3 %while.12 = (s32[]{:T(128)}, f32[1792,1792]{1,0:T(8,128)}, f32[224,49,256]{2,1,0:T(8,128)}, s32[]{:T(128)}, s32[512]{0:T(512)S(1)}, /*index=5*/bf16[2048,7,49]{2...) while((s32[]{:T(128)}, f32[1792,1792]{1,0:T(8,128)}, ...), condition=%wide.region_4.5_spmd, body=%wide.region_2.4_spmd.sunk | while | flops 3904316672 | bytes 142397968 | solution.py:103
  109.3 0.1 compare_select_fusion.5
  109.4 3.0 gather_fusion
  112.4 0.1 compare_select_fusion.6
  112.5 6.8 %gather_fusion.1 = bf16[256,49,256]{2,1,0:T(8,128)(2,1)} fusion(bf16[224,49,256]{2,1,0:T(8,128)(2,1)} %get-tuple-element.287, s32[1024]{0:T(1024)S(1)} %pad_clamp_fusion.7), kind=kCustom, calls=%fused_computation.1.clone.1 | custom fusion | bytes 12846080 | tf_op jit(solution)/shard_map/while/body/gather | solution.py:90
  119.3 0.1 dynamic_slice.20
  119.4 0.6 compare_convert_fusion.2
  120.0 0.9 convolution_multiply_fusion.2
  121.0 4.4 multiply_convert_fusion.2
  125.4 0.8 copy.47
  126.2 4.0 gather_fusion.2
  130.2 4.4 convolution_convert_fusion.2
  134.6 1.6 copy.48
  136.2 11.9 %convolution_add_fusion.2 = f32[1792,1792]{1,0:T(8,128)} fusion(f32[1792,1792]{1,0:T(8,128)} %get-tuple-element.263, bf16[256,1792]{0,1:T(8,128)(2,1)S(1)} %bitcast.57, bf16[256,1792]{0,1:T(8,128)(2,1)} %bitcast.58), kind=kOutput, calls=%fused_computation.4.clone.1 | convolution fusion | flops 1647378432 | bytes 27525120 | tf_op jit(solution)/shard_map/while/body/dot_general | solution.py:37
  148.1 4.7 fusion.49
  152.8 7.3 %fusion.50 = f32[256,49,256]{2,1,0:T(8,128)} fusion(bf16[256,7,49]{2,1,0:T(8,128)(2,1)S(1)} %gather_fusion, f32[256,7,256]{2,0,1:T(8,128)S(1)} %fusion.49, f32[256,256]{1,0:T(8,128)S(1)} %convolution_multiply_fusion.2), kind=kOutput, calls=%fused_computation.10.clone.1 | convolution fusion | flops 45875200 | bytes 15117824 | tf_op jit(solution)/shard_map/while/body/bij,bic->bjc/dot_general | solution.py:48
  160.1 49.3 %scatter_fusion = f32[224,49,256]{2,1,0:T(8,128)} fusion(f32[224,49,256]{2,1,0:T(8,128)} %get-tuple-element.264, s32[256]{0:T(256)S(1)} %get-tuple-element.242, f32[256,49,256]{2,1,0:T(8,128)} %fusion.50), kind=kCustom, calls=%fused_computation.3.clone.1 | custom fusion | flops 3211264 | bytes 38536192 | tf_op jit(solution)/shard_map/while/body/scatter-add | solution.py:96
  209.5 14.6 %copy.34 = f32[1,224,49,256]{3,0,2,1:T(1,128)} copy(f32[1,224,49,256]{3,2,1,0:T(8,128)} %bitcast.56) | data formatting | bytes 22478848 | tf_op jit(solution)/shard_map/broadcast_in_dim | solution.py:104
  224.1 0.0 all-reduce.4.cloned.1.call-start
  224.2 214.2 %reduce-scatter.2.cloned.1.call-done = f32[56,1792]{1,0:T(8,128)} async-done(((f32[1792,1792]{1,0:T(8,128)}), f32[56,1792]{1,0:T(8,128)}) %reduce-scatter.2.cloned.1.call-update) | async-done | bytes 401424 | tf_op jit(solution)/shard_map/reduce_scatter | solution.py:105
  438.4 0.6 dynamic-slice
  439.7 140.2 %all-reduce.6.cloned.1.call-done = f32[1,224,49,256]{3,0,2,1:T(1,128)} async-done(((f32[1,224,49,256]{3,0,2,1:T(1,128)}), f32[1,224,49,256]{3,0,2,1:T(1,128)}) %all-reduce.6.cloned.1.call-update) | async-done | bytes 11239440
  579.9 2.0 constant_dynamic-slice_fusion
  581.8 73.4 %all-reduce.4.cloned.1.call-done = f32[56,1792]{1,0:T(8,128)} async-done(((f32[56,1792]{1,0:T(8,128)}), f32[56,1792]{1,0:T(8,128)}) %all-reduce.4.cloned.1.call-update) | async-done | bytes 401424 | tf_op jit(solution)/shard_map/psum | solution.py:106
  655.2 1.8 copy.62
  (32 shorter events, 0.2 us)
Async XLA Ops:
  11.2 8.5 %copy-start.2 = (bf16[2048,7,49]{0,2,1:T(8,128)(2,1)S(1)}, bf16[2048,7,49]{0,2,1:T(8,128)(2,1)}, u32[]{:S(2)}) copy-start(bf16[2048,7,49]{0,2,1:T(8,128)(2,1)} %param.21) | copy-start | bytes 4214788
  11.2 12.8 %copy-start.5 = (s32[1,512]{1,0:T(1,128)S(1)}, s32[1,512]{1,0:T(1,128)}, u32[]{:S(2)}) copy-start(s32[1,512]{1,0:T(1,128)} %param.17) | copy-start | bytes 6148
  11.2 12.8 %copy-start.6 = (s32[1,512]{1,0:T(1,128)S(1)}, s32[1,512]{1,0:T(1,128)}, u32[]{:S(2)}) copy-start(s32[1,512]{1,0:T(1,128)} %param.16) | copy-start | bytes 6148
  11.2 12.8 %copy-start.7 = (s32[1,224]{1,0:T(1,128)S(1)}, s32[1,224]{1,0:T(1,128)}, u32[]{:S(2)}) copy-start(s32[1,224]{1,0:T(1,128)} %param.15) | copy-start | bytes 2692
  11.2 86.9 %all-to-all-start = ((bf16[32,1,7,49,256]{4,3,2,1,0:T(8,128)(2,1)}), bf16[32,1,7,49,256]{4,3,2,1,0:T(8,128)(2,1)}, u32[]{:S(2)}, u32[]{:S(2)}) async-start(bf16[32,1,7,49,256]{4,3,2,1,0:T(8,128)(2,1)} %stack.2), calls=%async_computation | async-start | bytes 12845056 | tf_op jit(solution)/shard_map/all_to_all | solution.py:77
  19.0 419.4 %reduce-scatter.2.cloned.1.call-start = ((), (), s32[]{:S(2)}) async-start(), calls=%async_computation.2 | async-start | bytes 13246464 | tf_op jit(solution)/shard_map/reduce_scatter | solution.py:105
  103.7 5.4 copy-start
  103.7 5.4 copy-start.3
  103.7 5.4 copy-start.4
  103.7 5.4 copy-start.8
  136.2 11.9 %copy-start.1 = (bf16[256,7,256]{0,2,1:T(8,128)(2,1)S(1)}, bf16[256,7,256]{0,2,1:T(8,128)(2,1)}, u32[]{:S(2)}) copy-start(bf16[256,7,256]{0,2,1:T(8,128)(2,1)} %copy.48) | copy-start | bytes 2752516 | tf_op jit(solution)/shard_map/while
  160.1 49.3 %copy-start.9 = (f32[600,256]{1,0:T(8,128)S(1)}, f32[600,256]{1,0:T(8,128)}, u32[]{:S(2)}) copy-start(f32[600,256]{1,0:T(8,128)} %get-tuple-element.332) | copy-start | bytes 1843204 | tf_op jit(solution)/shard_map/while
  209.5 370.4 %all-reduce.6.cloned.1.call-start = ((), (), s32[]{:S(2)}) async-start(), calls=%async_computation.4 | async-start | bytes 22478848
  224.1 214.3 %copy-start.10 = (u32[256]{0:T(256)S(1)}, u32[256]{0:T(256)}, u32[]{:S(2)}) copy-start(u32[256]{0:T(256)} %constant.58) | copy-start | bytes 3076
  224.1 431.1 %all-reduce.4.cloned.1.call-start = ((), (), s32[]{:S(2)}) async-start(), calls=%async_computation.3 | async-start | bytes 802816 | tf_op jit(solution)/shard_map/psum | solution.py:106
Sparse Core Ops, SparseCore 0:
  209.6 228.7 reduce-scatter.1
  441.9 137.9 all-reduce.5
  582.2 72.9 all-reduce.3
